TPU v7x, 512 devices: a whole 4x4x16 slice. The times are simulated.
512 devices in a mesh: ctx: 64 (over x, z), dp: 8 (over y, core).
Axes of the slice: x: 4, y: 4, z: 16, core: 2. Of those that a mesh axis runs over, the one named last changes fastest.
Arguments:
- queries: bfloat16 [24576, 8192], P(('ctx', 'dp')), may hold values from -8 to 8
- keys: bfloat16 [24576, 1024], P('ctx', 'dp'), may hold values from -4 to 4
- values: bfloat16 [24576, 1024], P('ctx', 'dp'), may hold values from -6 to 6
- block_list: int32 [192, 13], P('ctx'), may hold values from 0 to 191, as said below
Outputs:
- attended: bfloat16 [24576, 8192], P(('ctx', 'dp'))
Inputs may be any that keep to these rules, and one draw needn't show every extreme that they name: `block_list`: entries 0 to 2 of row n are n - 1, n and n + 1 modulo 192; entries 3 and 4 are 0 and 1; entries 5 to 12 are random blocks. The random blocks listed by the 3 query blocks of one context shard lie in other shards, at most 1 of them in any one shard, and exactly 1 in some shard.
All inputs are finite; a program needn't handle non-finite values.
Results may differ from a plain program's by a relative error of at most 0.0049.
Values may be sent and summed in bfloat16 or wider, within the bound.
A program may use at most 128 MiB of HBM per device.

v0:
```python
import math

import jax
import jax.numpy as jnp
from jax import lax
from jax.sharding import PartitionSpec as P

HEADS = 64
KV_HEADS = 8
HEAD_DIM = 128
BLOCK = 128
LIST = 13


def shards(queries, keys, values, block_list):
    head_rows = lax.all_to_all(queries, "dp", split_axis=1, concat_axis=0, tiled=True)
    span = keys.shape[0]
    kv_width = keys.shape[1]
    kv_heads = kv_width // HEAD_DIM
    group_size = HEADS // KV_HEADS
    blocks_here = span // BLOCK
    full_width = 2 * kv_width
    kv_local = jnp.concatenate([keys, values], axis=1)
    gathered = lax.all_gather(kv_local, "ctx", axis=0, tiled=True)
    total_blocks = gathered.shape[0] // BLOCK
    flat_cache = gathered.reshape(total_blocks, BLOCK * full_width)
    block_ids = block_list.reshape(-1)
    selector = (block_ids[:, None] == jnp.arange(total_blocks, dtype=jnp.int32)[None, :]).astype(
        jnp.bfloat16
    )
    picked = jnp.dot(selector, flat_cache, preferred_element_type=jnp.float32).astype(jnp.bfloat16)
    picked = picked.reshape(blocks_here, LIST, BLOCK, full_width)
    score_scale = 1.0 / math.sqrt(HEAD_DIM)
    earlier = jnp.arange(LIST)[:, None] > jnp.arange(LIST)[None, :]
    query_blocks = head_rows.reshape(blocks_here, BLOCK, kv_heads, group_size, HEAD_DIM)

    def one_block(inputs):
        q_block, block_keys, block_ids = inputs
        repeats = (block_ids[:, None] == block_ids[None, :]) & earlier
        keep_block = jnp.logical_not(jnp.any(repeats, axis=1))
        key_mask = jnp.repeat(keep_block, BLOCK)
        key_rows = block_keys[:, :, :kv_width].reshape(LIST * BLOCK, kv_heads, HEAD_DIM)
        value_rows = block_keys[:, :, kv_width:].reshape(LIST * BLOCK, kv_heads, HEAD_DIM)
        scores = (
            jnp.einsum("tkgd,skd->kgts", q_block, key_rows, preferred_element_type=jnp.float32)
            * score_scale
        )
        row_max = jnp.max(jnp.where(key_mask, scores, -jnp.inf), axis=-1, keepdims=True)
        unnormed = jnp.where(key_mask, jnp.exp(scores - row_max), 0.0)
        row_sum = jnp.sum(unnormed, axis=-1, keepdims=True)
        weights = (unnormed / row_sum).astype(jnp.bfloat16)
        result = jnp.einsum(
            "kgts,skd->tkgd", weights, value_rows, preferred_element_type=jnp.float32
        )
        return result.astype(jnp.bfloat16).reshape(BLOCK, kv_heads * group_size * HEAD_DIM)

    attended = lax.map(one_block, (query_blocks, picked, block_list))
    attended = attended.reshape(blocks_here * BLOCK, kv_heads * group_size * HEAD_DIM)
    return lax.all_to_all(attended, "dp", split_axis=0, concat_axis=1, tiled=True)


def solution(mesh):
    in_specs = (P(("ctx", "dp"), None), P("ctx", "dp"), P("ctx", "dp"), P("ctx", None))
    out_specs = P(("ctx", "dp"), None)
    return jax.shard_map(shards, mesh=mesh, in_specs=in_specs, out_specs=out_specs, check_vma=False)
```

profile of v0, /device:TPU:1, one launch (start us, length us, event | category | flops | bytes accessed | tf_op | source)
XLA Modules:
  0.0 263.0 jit_solution(17403467561798822007)
XLA Ops:
  6.5 0.0 all-gather.2.cloned.1.call-start
  6.5 1.6 pad_maximum_fusion
  8.2 0.0 all-gather.2.cloned.1.call-update
  8.2 2.1 copy.39
  10.3 10.3 %all-to-all-start = ((bf16[48,8,1024]{2,0,1:T(8,128)(2,1)}), bf16[48,8,1024]{2,0,1:T(8,128)(2,1)S(1)}, u32[]{:S(2)}, u32[]{:S(2)}) async-start(bf16[48,8,1024]{2,0,1:T(8,128)(2,1)} %bitcast.67), calls=%async_computation | async-start | bytes 1572864 | tf_op jit(solution)/shard_map/all_to_all | solution.py:16
  20.7 0.8 eq.30
  21.4 11.5 %all-to-all-done = bf16[48,8,1024]{2,0,1:T(8,128)(2,1)S(1)} async-done(((bf16[48,8,1024]{2,0,1:T(8,128)(2,1)}), bf16[48,8,1024]{2,0,1:T(8,128)(2,1)S(1)}, u32[]{:S(2)}, u32[]{:S(2)}) %all-to-all-start) | async-done | bytes 786464 | tf_op jit(solution)/shard_map/all_to_all | solution.py:16
  33.0 1.1 copy.33
  34.1 150.5 %all-gather.2.cloned.1.call-done = bf16[24576,256]{1,0:T(8,128)(2,1)} async-done(((bf16[384,256]{1,0:T(8,128)(2,1)}), bf16[24576,256]{1,0:T(8,128)(2,1)}) %all-gather.2.cloned.1.call-update) | async-done | bytes 12582928 | tf_op jit(solution)/shard_map/all_gather | solution.py:24
  184.6 19.5 %reshape.58 = bf16[192,32768]{1,0:T(8,128)(2,1)} reshape(bf16[24576,256]{1,0:T(8,128)(2,1)} %all-gather.2.cloned.1.call-done) | data formatting | bytes 25165824 | tf_op jit(solution)/shard_map/reshape | solution.py:26
  204.1 6.9 %convolution_convert_fusion = bf16[39,32768]{1,0:T(8,128)(2,1)S(1)} fusion(bf16[192,32768]{1,0:T(8,128)(2,1)} %reshape.58, s32[39]{0:T(128)S(1)} %eq.30), kind=kOutput, calls=%fused_computation.24 | convolution fusion | flops 492019008 | bytes 15138972 | tf_op jit(solution)/shard_map/dot_general | solution.py:31
  211.0 0.6 copy.32
  211.6 0.2 slice.10
  211.8 24.2 %while.11 = (s32[]{:T(128)}, bf16[3,128,1024]{2,1,0:T(8,128)(2,1)}, bf16[3,13,128,256]{3,2,1,0:T(8,128)(2,1)S(1)}, s32[3,13]{1,0:T(4,128)}, bf16[3,128,1,8,128]{4,3,1,0,2:T(8,128)(2,1)}, /*index=5*/s32[]{:T(128)}) while((s32[]{:T(128)}, bf16[3,128,1024]{2,1,0:T(8,128)(2,1)}, bf16[3,13,128,256]{3,2,1,0:T(8,128)(2,1)S(1)}, ...), condition=%wide.region_4.5_spmd.clone, body=%wide.region_0.4_spmd.clone.sunk | while | flops 892992128 | bytes 26832160 | solution.py:57
  211.8 0.7 fusion.35
  212.5 0.2 fusion.36
  212.7 0.1 broadcast_bitcast_fusion.2
  212.8 0.1 dynamic-slice_bitcast_fusion.2
  212.8 0.2 fusion.34
  213.1 1.0 constant_dynamic-slice_fusion.3
  214.1 1.1 fusion.37
  215.1 1.9 fusion.38
  217.1 1.9 fusion.39
  219.0 0.1 copy.43
  219.2 0.7 constant_dynamic-update-slice_fusion.2
  219.9 0.7 fusion.35
  220.6 0.2 fusion.36
  220.8 0.1 broadcast_bitcast_fusion.2
  220.8 0.1 dynamic-slice_bitcast_fusion.2
  220.9 0.2 fusion.34
  221.1 1.0 constant_dynamic-slice_fusion.3
  222.1 1.1 fusion.37
  223.2 1.9 fusion.38
  225.1 1.9 fusion.39
  227.1 0.1 copy.43
  227.2 0.7 constant_dynamic-update-slice_fusion.2
  227.9 0.7 fusion.35
  228.6 0.2 fusion.36
  228.8 0.1 broadcast_bitcast_fusion.2
  228.9 0.1 dynamic-slice_bitcast_fusion.2
  229.0 0.2 fusion.34
  229.2 1.0 constant_dynamic-slice_fusion.3
  230.2 1.1 fusion.37
  231.3 1.9 fusion.38
  233.2 1.9 fusion.39
  235.1 0.1 copy.43
  235.3 0.7 constant_dynamic-update-slice_fusion.2
  236.0 19.2 %all_to_all.35 = bf16[8,48,1024]{2,1,0:T(8,128)(2,1)S(1)} all-to-all(bf16[8,48,1024]{2,1,0:T(8,128)(2,1)} %bitcast.103), channel_id=1, replica_groups=mesh['ctx'=64,'dp'=8] {'dp'}, dimensions={0} | all-to-all | bytes 1572864 | tf_op jit(solution)/shard_map/all_to_all | solution.py:59
  255.2 0.9 copy.31
  (4 shorter events, 0.0 us)
Async XLA Ops:
  6.5 178.0 %all-gather.2.cloned.1.call-start = ((), (), s32[]{:S(2)}) async-start(), calls=%async_computation.2 | async-start | bytes 12779520 | tf_op jit(solution)/shard_map/all_gather | solution.py:24
  10.3 22.6 %all-to-all-start = ((bf16[48,8,1024]{2,0,1:T(8,128)(2,1)}), bf16[48,8,1024]{2,0,1:T(8,128)(2,1)S(1)}, u32[]{:S(2)}, u32[]{:S(2)}) async-start(bf16[48,8,1024]{2,0,1:T(8,128)(2,1)} %bitcast.67), calls=%async_computation | async-start | bytes 1572864 | tf_op jit(solution)/shard_map/all_to_all | solution.py:16
Sparse Core Ops, SparseCore 0:
  10.3 174.2 all-gather.1
where the time goes:
time: 264 us; the launch traced here: 263 us
  waiting for transfers between devices  162 us (61%)
  local copies, waits for them, and re-layouts  34 us (13%)
  blocking collectives  19.2 us (7%)
  matrix products  15.9 us (6%)
  between operations  13.4 us (5%)
  starting transfers between devices  10.3 us (4%)
  other arithmetic  8.04 us (3%)
    all_gather x1, waiting for transfers between devices, shards(): gathered = lax.all_gather(kv_local, 'ctx', axis=0, tiled=True)  150 us
    reshape x1, local copies, waits for them, and re-layouts, shards(): flat_cache = gathered.reshape(total_blocks, BLOCK * full_width)  19.5 us
    all_to_all x1, blocking collectives, shards(): lax.all_to_all(attended, 'dp', split_axis=0, concat_axis=1, tiled=True)  19.2 us
    all_to_all x1, waiting for transfers between devices, shards(): lax.all_to_all(queries, 'dp', split_axis=1, concat_axis=0, tiled=True)  11.5 us
    all_to_all x1, starting transfers between devices, shards(): lax.all_to_all(queries, 'dp', split_axis=1, concat_axis=0, tiled=True)  10.3 us
    dot_general x1, matrix products, shards(): jnp.dot(selector, flat_cache, preferred_element_type=jnp.float32)  6.9 us
    reduce_sum x3, other arithmetic, one_block(): row_sum = jnp.sum(unnormed, axis=-1, keepdims=True)  5.8 us
    dot_general x3, matrix products, one_block(): jnp.einsum('kgts,skd->tkgd', weights, value_rows, preferred_element_type=...  5.77 us
  transfers between devices with their start and end apart: 2, of which 2 were waited for; matrix products, arithmetic and copies ran while one was open for 2% of the time, Pallas kernels for 0%

commit v1 on v0

v1 whole, which is shorter than its diff:
```python
import math

import jax
import jax.numpy as jnp
from jax import lax
from jax.experimental import pallas as pl
from jax.experimental.pallas import tpu as pltpu
from jax.sharding import PartitionSpec as P

HEAD_DIM = 128
BLOCK = 128
LIST = 13
KB = 3
GROUP = 8
NX, NZ, NDP = 4, 16, 8
TOK = 48
WIDTH = GROUP * HEAD_DIM
SPAN = KB * BLOCK
OWN = NZ * KB
RECV = OWN
GLOB = RECV + NX * NZ
EDGE = GLOB + 2
SLOTS = EDGE + 1
PAIR = 2
STEPS = GROUP // PAIR
MESH = pl.DeviceIdType.MESH


def kernel(list_ref, q_ref, k_ref, v_ref, out_ref, kv, picked, kcat, vcat, qbuf, obuf, ask, asked, asked_s,
           load_sem, own_q_sem, own_out_sem, ask_send, ask_recv, asked_sem, q_send, q_recv, z_send, z_half_send, z_recv,
           z_half_recv, x_send, x_recv, glob_send, glob_recv, edge_send, edge_recv, out_send, out_recv):
    c = lax.axis_index("ctx")
    p = lax.axis_index("dp")
    x = c // NZ
    z = c % NZ

    def at_x(d):
        return {"ctx": lax.rem(x + d, NX) * NZ + z, "dp": p}

    def at_z(d):
        return {"ctx": x * NZ + lax.rem(z + d, NZ), "dp": p}

    def at_p(d):
        return {"ctx": c, "dp": lax.rem(p + d, NDP)}

    def send(src, dst, ssem, rsem, dev):
        return pltpu.make_async_remote_copy(
            src_ref=src, dst_ref=dst, send_sem=ssem, recv_sem=rsem, device_id=dev, device_id_type=MESH
        )

    barrier = pltpu.get_barrier_semaphore()
    for d in range(1, NX):
        pl.semaphore_signal(barrier, inc=1, device_id=at_x(d), device_id_type=MESH)
    for d in (1, NZ - 1):
        pl.semaphore_signal(barrier, inc=1, device_id=at_z(d), device_id_type=MESH)
    for d in range(1, NDP):
        pl.semaphore_signal(barrier, inc=1, device_id=at_p(d), device_id_type=MESH)

    loads = []
    for b in range(KB):
        slot = z * KB + b
        loads.append(pltpu.make_async_copy(k_ref.at[b], kv.at[slot, pl.ds(0, BLOCK)], load_sem.at[0, b]))
        loads.append(pltpu.make_async_copy(v_ref.at[b], kv.at[slot, pl.ds(BLOCK, BLOCK)], load_sem.at[1, b]))
    for copy in loads:
        copy.start()
    own_q = pltpu.make_async_copy(
        q_ref.at[:, pl.ds(pl.multiple_of(p * WIDTH, WIDTH), WIDTH)],
        qbuf.at[pl.ds(pl.multiple_of(p * TOK, 16), TOK)], own_q_sem)
    own_q.start()

    rows = lax.broadcasted_iota(jnp.int32, (NX * NZ, 128), 0) * KB
    wanted = jnp.zeros((NX * NZ, 128), jnp.int32)
    for i in range(KB):
        for e in range(5, LIST):
            off = list_ref[i, e] - rows
            wanted = wanted + jnp.where(off == 1, 1, 0) + jnp.where(off == 2, 2, 0)
    ask[...] = wanted.reshape(NX, NZ, 128)

    for copy in loads:
        copy.wait()
    pl.semaphore_wait(barrier, NX - 1 + 2 + NDP - 1)

    asks = []
    for d in range(1, NX):
        asks.append(send(ask.at[lax.rem(x + d, NX)], asked.at[d], ask_send.at[d], ask_recv.at[d], at_x(d)))
        asks[-1].start()

    def z_block(slot, up, k, b):
        way = 0 if up else 1
        s = slot * KB + b
        return send(kv.at[s], kv.at[s], z_send.at[way], z_recv.at[way, k, b], at_z(1 if up else NZ - 1))

    def z_half(slot, up, b):
        way = 0 if up else 1
        s = slot * KB + b
        part = pl.ds(0 if up else BLOCK, BLOCK)
        return send(kv.at[s, part], kv.at[s, part], z_half_send.at[way], z_half_recv.at[way, b],
                    at_z(1 if up else NZ - 1))

    for b in range(KB):
        for up in (True, False):
            z_block(z, up, 1, b).start()

    q_copies = []
    for d in range(1, NDP):
        t = lax.rem(p + d, NDP)
        q_copies.append(send(
            q_ref.at[:, pl.ds(pl.multiple_of(t * WIDTH, WIDTH), WIDTH)],
            qbuf.at[pl.ds(pl.multiple_of(p * TOK, 16), TOK)],
            q_send.at[d], q_recv.at[d], at_p(d)))
        q_copies[-1].start()

    for copy in asks:
        copy.wait()
    to_scalars = pltpu.make_async_copy(asked, asked_s, asked_sem)
    to_scalars.start()
    to_scalars.wait()

    def glob_copy(d):
        return send(kv.at[pl.ds(0, 2)], kv.at[pl.ds(GLOB, 2)], glob_send.at[d], glob_recv, at_x(d))

    def edge_copy(slot, d):
        return send(kv.at[slot], kv.at[EDGE], edge_send, edge_recv, at_x(d))

    def share(slot):
        first, second, third = (kv[slot * KB + b] for b in range(KB))
        for d in (2, 1, 3):
            off = asked_s[NX - d, slot, 0]
            picked[d - 1, slot] = jnp.where(off == 1, second, jnp.where(off == 2, third, first))
            send(picked.at[d - 1, slot], kv.at[RECV + x * NZ + slot], x_send.at[d - 1], x_recv.at[d - 1],
                 at_x(d)).start()

        @pl.when((x == 0) & (slot == 0))
        def _():
            for d in range(1, NX):
                glob_copy(d).start()

        @pl.when((z == 0) & (slot == NZ - 1))
        def _():
            edge_copy((NZ - 1) * KB + KB - 1, 1).start()

        @pl.when((z == NZ - 1) & (slot == 0))
        def _():
            edge_copy(0, NX - 1).start()

    share(z)

    @pl.loop(1, NZ // 2)
    def _(k):
        above = lax.rem(z + NZ - k, NZ)
        below = lax.rem(z + k, NZ)
        for b in range(KB):
            for up, slot in ((True, above), (False, below)):
                z_block(slot, up, k, b).wait_recv()

                @pl.when(k < NZ // 2 - 1)
                def _():
                    z_block(slot, up, k + 1, b).start()

                @pl.when(k == NZ // 2 - 1)
                def _():
                    z_half(slot, up, b).start()

        share(above)
        share(below)

    far = lax.rem(z + NZ // 2, NZ)
    for b in range(KB):
        for up in (True, False):
            z_half(far, up, b).wait_recv()
    share(far)

    for copy in q_copies:
        copy.wait()
    own_q.wait()

    for d in range(1, NX):
        source = lax.rem(x + NX - d, NX)
        landed = kv.at[pl.ds(RECV + source * NZ, NZ)]
        send(picked.at[d - 1], landed, x_send.at[d - 1], x_recv.at[d - 1], at_x(d)).wait()

    @pl.when(x != 0)
    def _():
        glob_copy(1).wait_recv()

    @pl.when((z == 0) | (z == NZ - 1))
    def _():
        edge_copy(0, 1).wait()

    for i in range(KB):
        slots = []
        if i == 0:
            slots.append(jnp.where(z == 0, EDGE, z * KB - 1))
        else:
            slots.append(z * KB + i - 1)
        slots.append(z * KB + i)
        if i == KB - 1:
            slots.append(jnp.where(z == NZ - 1, EDGE, z * KB + KB))
        else:
            slots.append(z * KB + i + 1)
        for g in range(2):
            slots.append(jnp.where(x == 0, g, GLOB + g))
        for e in range(5, LIST):
            block = list_ref[i, e]
            shard = (block * 21846) >> 16
            here = (shard >> 4) == x
            slots.append(jnp.where(here, (shard & 15) * KB + block - shard * KB, RECV + shard))
        for e in range(LIST):
            again = jnp.int32(0)
            for f in range(e):
                again = again | jnp.where(list_ref[i, e] == list_ref[i, f], 1, 0)
            keep = jnp.where(again == 1, 0.0, 1.0)
            both = kv[slots[e]]
            kcat[i, pl.ds(e * BLOCK, BLOCK)] = both[:BLOCK]
            mask = jnp.full((BLOCK, HEAD_DIM), keep, jnp.float32).astype(jnp.bfloat16)
            vcat[i, pl.ds(e * BLOCK, BLOCK), pl.ds(0, HEAD_DIM)] = both[BLOCK:] * mask
            vcat[i, pl.ds(e * BLOCK, BLOCK), pl.ds(HEAD_DIM, HEAD_DIM)] = mask

    factor = math.log2(math.e) / math.sqrt(HEAD_DIM)

    def out_copy(d, step):
        t = lax.rem(p + d, NDP)
        return send(
            obuf.at[pl.ds(pl.multiple_of(t * TOK, 16), TOK), pl.ds(pl.multiple_of(step * PAIR * HEAD_DIM, 256), PAIR * HEAD_DIM)],
            out_ref.at[:, pl.ds(pl.multiple_of(p * WIDTH + step * PAIR * HEAD_DIM, 256), PAIR * HEAD_DIM)],
            out_send, out_recv, at_p(d))

    @pl.loop(0, STEPS)
    def _(step):
        for i in range(KB):
            tok = pl.ds(i * BLOCK, BLOCK)
            cols = [pl.ds(pl.multiple_of((step * PAIR + h) * HEAD_DIM, HEAD_DIM), HEAD_DIM) for h in range(PAIR)]
            q = jnp.concatenate([qbuf[tok, col] for col in cols], axis=0)
            scores = lax.dot_general(q, kcat[i], (((1,), (1,)), ((), ())), preferred_element_type=jnp.float32)
            row_max = jnp.max(scores, axis=-1, keepdims=True)
            unnormed = jnp.exp2((scores - row_max) * factor).astype(jnp.bfloat16)
            result = jnp.dot(unnormed, vcat[i], preferred_element_type=jnp.float32)
            result = (result[:, :HEAD_DIM] / result[:, HEAD_DIM:]).astype(jnp.bfloat16)
            for h in range(PAIR):
                obuf[tok, cols[h]] = result[h * BLOCK:(h + 1) * BLOCK]
        for d in range(1, NDP):
            out_copy(d, step).start()

    own_out = pltpu.make_async_copy(
        obuf.at[pl.ds(pl.multiple_of(p * TOK, 16), TOK)],
        out_ref.at[:, pl.ds(pl.multiple_of(p * WIDTH, WIDTH), WIDTH)], own_out_sem)
    own_out.start()
    own_out.wait()

    for way in range(2):
        up = way == 0
        dev = at_z(1 if up else NZ - 1)
        full = kv.at[pl.ds(0, (NZ // 2 - 1) * KB)]
        send(full, full, z_send.at[way], z_recv.at[way, 1, 0], dev).wait_send()
        half = kv.at[pl.ds(0, KB), pl.ds(0, BLOCK)]
        send(half, half, z_half_send.at[way], z_recv.at[way, 1, 0], dev).wait_send()

    @pl.when(x == 0)
    def _():
        for d in range(1, NX):
            glob_copy(d).wait_send()

    everything = out_ref.at[:, pl.ds(0, (NDP - 1) * WIDTH)]
    send(everything, everything, out_send, out_recv, at_p(1)).wait()


def shards(queries, keys, values, block_list):
    dma = pltpu.SemaphoreType.DMA
    bf16 = jnp.bfloat16
    hbm = pl.BlockSpec(memory_space=pl.ANY)
    return pl.pallas_call(
        kernel,
        out_shape=jax.ShapeDtypeStruct(queries.shape, queries.dtype),
        in_specs=[pl.BlockSpec(memory_space=pltpu.SMEM), hbm, hbm, hbm],
        out_specs=hbm,
        scratch_shapes=[
            pltpu.VMEM((SLOTS, 2 * BLOCK, HEAD_DIM), bf16),
            pltpu.VMEM((NX - 1, NZ, 2 * BLOCK, HEAD_DIM), bf16),
            pltpu.VMEM((KB, LIST * BLOCK, HEAD_DIM), bf16),
            pltpu.VMEM((KB, LIST * BLOCK, 2 * HEAD_DIM), bf16),
            pltpu.VMEM((SPAN, WIDTH), bf16),
            pltpu.VMEM((SPAN, WIDTH), bf16),
            pltpu.VMEM((NX, NZ, 128), jnp.int32),
            pltpu.VMEM((NX, NZ, 128), jnp.int32),
            pltpu.SMEM((NX, NZ, 128), jnp.int32),
            dma((2, KB)), dma, dma, dma((NX,)), dma((NX,)), dma, dma((NDP,)), dma((NDP,)),
            dma((2,)), dma((2,)), dma((2, NZ // 2, KB)), dma((2, KB)),
            dma((NX - 1,)), dma((NX - 1,)), dma((NX,)), dma, dma, dma, dma, dma,
        ],
        compiler_params=pltpu.CompilerParams(
            collective_id=0, has_side_effects=True, vmem_limit_bytes=48 * 1024 * 1024
        ),
        name="gather_attend",
    )(block_list, queries, keys.reshape(KB, BLOCK, HEAD_DIM), values.reshape(KB, BLOCK, HEAD_DIM))


def solution(mesh):
    in_specs = (P(("ctx", "dp"), None), P("ctx", "dp"), P("ctx", "dp"), P("ctx", None))
    out_specs = P(("ctx", "dp"), None)
    return jax.shard_map(shards, mesh=mesh, in_specs=in_specs, out_specs=out_specs, check_vma=False)
```

time: 264 us -> 90.5 us (0.34)
  waiting for transfers between devices: 162 us -> 0 us
  Pallas kernels: 0 us -> 85.6 us
  local copies, waits for them, and re-layouts: 34 us -> 4.48 us
  blocking collectives: 19.2 us -> 0 us
  matrix products: 15.9 us -> 0 us
  between operations: 13.4 us -> 0.01 us
  starting transfers between devices: 10.3 us -> 0 us
  other arithmetic: 8.04 us -> 0 us
    all_gather x1 -> x0, waiting for transfers between devices: 150 us -> none  [shards(): gathered = lax.all_gather(kv_local, 'ctx', axis=0, tiled=True)]
    pallas_call x0 -> x1, Pallas kernels: none -> 85.6 us  [shards(): pl.pallas_call(kernel, out_shape=jax.ShapeDtypeStruct(queries.shape, quer...]
    reshape x4 -> x0, local copies, waits for them, and re-layouts: 19.8 us -> none  [the longest x1 19.5 us: shards(): flat_cache = gathered.reshape(total_blocks, BLOCK * full_width)]
    all_to_all x1 -> x0, blocking collectives: 19.2 us -> none  [shards(): lax.all_to_all(attended, 'dp', split_axis=0, concat_axis=1, tiled=True)]
    dot_general x7 -> x0, matrix products: 15.9 us -> none  [the longest x1 6.9 us: shards(): jnp.dot(selector, flat_cache, preferred_element_type=jnp.float32)]
    all_to_all x1 -> x0, waiting for transfers between devices: 11.5 us -> none  [shards(): lax.all_to_all(queries, 'dp', split_axis=1, concat_axis=0, tiled=True)]
    all_to_all x1 -> x0, starting transfers between devices: 10.3 us -> none  [shards(): lax.all_to_all(queries, 'dp', split_axis=1, concat_axis=0, tiled=True)]
    reduce_sum x3 -> x0, other arithmetic: 5.8 us -> none  [one_block(): row_sum = jnp.sum(unnormed, axis=-1, keepdims=True)]
  transfers between devices with their start and end apart: 2 -> 0, of which waited for: 2 -> 0; matrix products, arithmetic and copies ran while one was open for 2% -> 0% of each run, Pallas kernels for 0% -> 0%
where the time goes in v1:
time: 90.5 us; the launch traced here: 90.1 us
  Pallas kernels  85.6 us (95%)
  local copies, waits for them, and re-layouts  4.48 us (5%)
    pallas_call x1, Pallas kernels, shards(): pl.pallas_call(kernel, out_shape=jax.ShapeDtypeStruct(queries.shape, quer...  85.6 us
    unnamed x9, local copies, waits for them, and re-layouts  4.48 us

profile of v1, /device:TPU:1, one launch (start us, length us, event | category | flops | bytes accessed | tf_op | source)
XLA Modules:
  0.0 90.1 jit_solution(1622822124201204062)
XLA Ops:
  0.0 0.0 copy-start.3
  0.0 0.7 copy-done.3
  0.7 0.0 copy-start
  0.7 1.1 %copy-done = bf16[48,8192]{1,0:T(8,128)(2,1)S(1)} copy-done((bf16[48,8192]{1,0:T(8,128)(2,1)S(1)}, bf16[48,8192]{1,0:T(8,128)(2,1)}, u32[]{:S(2)}) %copy-start) | copy-done | bytes 786456
  1.8 0.0 copy-start.1
  1.8 0.9 copy-done.1
  2.7 0.0 copy-start.2
  2.7 0.9 copy-done.2
  3.6 85.6 %gather_attend.1 = bf16[48,8192]{1,0:T(8,128)(2,1)S(1)} custom-call(s32[3,13]{1,0:T(4,128)S(1)} %copy-done.3, bf16[48,8192]{1,0:T(8,128)(2,1)S(1)} %copy-done, bf16[3,128,128]{2,1,0:T(8,128)(2,1)S(1)} %bitcast.2, bf16[3,128,128]{2,1,0:T(8,128)(2,1)S(1)} %bitcast.3), custom_call_target="tpu_custom_call" | custom-call | tf_op jit(solution)/shard_map/gather_attend/pallas_call | solution.py:271
  89.3 0.9 copy.6
Async XLA Ops:
  0.0 0.7 copy-start.3
  0.7 1.1 %copy-start = (bf16[48,8192]{1,0:T(8,128)(2,1)S(1)}, bf16[48,8192]{1,0:T(8,128)(2,1)}, u32[]{:S(2)}) copy-start(bf16[48,8192]{1,0:T(8,128)(2,1)} %q_ref.1) | copy-start | bytes 2359300
  1.8 0.9 copy-start.1
  2.7 0.9 copy-start.2

commit v2 on v1

--- a/solution.py
+++ b/solution.py
@@ -20,15 +20,17 @@
 RECV = OWN
 GLOB = RECV + NX * NZ
 EDGE = GLOB + 2
-SLOTS = EDGE + 1
+NEAR = 2
+OPP = EDGE + 1
+SLOTS = OPP + (2 * NEAR + 1) * KB
 PAIR = 2
 STEPS = GROUP // PAIR
 MESH = pl.DeviceIdType.MESH
 
 
-def kernel(list_ref, q_ref, k_ref, v_ref, out_ref, kv, picked, kcat, vcat, qbuf, obuf, ask, asked, asked_s,
+def kernel(list_ref, q_ref, k_ref, v_ref, out_ref, kv, picked, kcat, vcat, qbuf, obuf, ask, asked, asked_s, lower_in,
            load_sem, own_q_sem, own_out_sem, ask_send, ask_recv, asked_sem, q_send, q_recv, z_send, z_half_send, z_recv,
-           z_half_recv, x_send, x_recv, glob_send, glob_recv, edge_send, edge_recv, out_send, out_recv):
+           z_half_recv, x_send, x_recv, glob_send, glob_recv, opp_send, opp_recv, edge_send, edge_recv, out_send, out_recv):
     c = lax.axis_index("ctx")
     p = lax.axis_index("dp")
     x = c // NZ
@@ -51,8 +53,7 @@
     barrier = pltpu.get_barrier_semaphore()
     for d in range(1, NX):
         pl.semaphore_signal(barrier, inc=1, device_id=at_x(d), device_id_type=MESH)
-    for d in (1, NZ - 1):
-        pl.semaphore_signal(barrier, inc=1, device_id=at_z(d), device_id_type=MESH)
+    pl.semaphore_signal(barrier, inc=1, device_id=at_z(NZ - 1), device_id_type=MESH)
     for d in range(1, NDP):
         pl.semaphore_signal(barrier, inc=1, device_id=at_p(d), device_id_type=MESH)
 
@@ -78,7 +79,8 @@
 
     for copy in loads:
         copy.wait()
-    pl.semaphore_wait(barrier, NX - 1 + 2 + NDP - 1)
+    pl.semaphore_wait(barrier, NX - 1 + 1 + NDP - 1)
+    pl.semaphore_signal(lower_in, inc=1, device_id=at_z(1), device_id_type=MESH)
 
     asks = []
     for d in range(1, NX):
@@ -98,8 +100,19 @@
                     at_z(1 if up else NZ - 1))
 
     for b in range(KB):
-        for up in (True, False):
-            z_block(z, up, 1, b).start()
+        z_block(z, True, 1, b).start()
+
+    def opp_block(way, hop, b):
+        row = -hop if way == 0 else hop
+        step = -1 if way == 0 else 1
+        return send(kv.at[OPP + (row + NEAR) * KB + b], kv.at[OPP + (row + step + NEAR) * KB + b],
+                    opp_send.at[way], opp_recv.at[way, hop + 1, b], at_z(1 if way == 0 else NZ - 1))
+
+    def opp_first(b):
+        return send(kv.at[z * KB + b], kv.at[OPP + NEAR * KB + b], opp_send.at[2], opp_recv.at[0, 0, b], at_x(2))
+
+    for b in range(KB):
+        opp_first(b).start()
 
     q_copies = []
     for d in range(1, NDP):
@@ -110,6 +123,13 @@
             q_send.at[d], q_recv.at[d], at_p(d)))
         q_copies[-1].start()
 
+    def start_down():
+        pl.semaphore_wait(lower_in, 1)
+        for b in range(KB):
+            z_block(z, False, 1, b).start()
+
+    pl.when(z != 0)(start_down)
+
     for copy in asks:
         copy.wait()
     to_scalars = pltpu.make_async_copy(asked, asked_s, asked_sem)
@@ -119,21 +139,29 @@
     def glob_copy(d):
         return send(kv.at[pl.ds(0, 2)], kv.at[pl.ds(GLOB, 2)], glob_send.at[d], glob_recv, at_x(d))
 
+    def glob_on(way):
+        both = kv.at[pl.ds(GLOB, 2)]
+        return send(both, both, glob_send.at[way], glob_recv, at_z(1 if way == 0 else NZ - 1))
+
+    up_on = (x != 0) & (z < NZ // 2)
+    down_on = (x != 0) & ((z == 0) | (z > NZ // 2 + 1))
+
     def edge_copy(slot, d):
         return send(kv.at[slot], kv.at[EDGE], edge_send, edge_recv, at_x(d))
 
-    def share(slot):
+    def share(slot, dests, edges=True):
         first, second, third = (kv[slot * KB + b] for b in range(KB))
-        for d in (2, 1, 3):
+
+        def give(d):
             off = asked_s[NX - d, slot, 0]
             picked[d - 1, slot] = jnp.where(off == 1, second, jnp.where(off == 2, third, first))
             send(picked.at[d - 1, slot], kv.at[RECV + x * NZ + slot], x_send.at[d - 1], x_recv.at[d - 1],
                  at_x(d)).start()
 
-        @pl.when((x == 0) & (slot == 0))
-        def _():
-            for d in range(1, NX):
-                glob_copy(d).start()
+        for d in dests:
+            give(d)
+        if not edges:
+            return
 
         @pl.when((z == 0) & (slot == NZ - 1))
         def _():
@@ -143,7 +171,19 @@
         def _():
             edge_copy(0, NX - 1).start()
 
-    share(z)
+    @pl.when((x == 0) & (z == 0))
+    def _():
+        for d in range(1, NX):
+            glob_copy(d).start()
+
+    share(z, (1, 3))
+    pl.when(z == 0)(start_down)
+
+    @pl.when((x != 0) & (z == 0))
+    def _():
+        glob_copy(1).wait_recv()
+        glob_on(0).start()
+        glob_on(1).start()
 
     @pl.loop(1, NZ // 2)
     def _(k):
@@ -161,14 +201,42 @@
                 def _():
                     z_half(slot, up, b).start()
 
-        share(above)
-        share(below)
+        @pl.when((x != 0) & ((above == 0) | (below == 0)) & (z != NZ // 2))
+        def _():
+            glob_copy(1).wait_recv()
+            pl.when(up_on)(lambda: glob_on(0).start())
+            pl.when(down_on)(lambda: glob_on(1).start())
+
+        @pl.when(k <= NEAR)
+        def _():
+            share(above, (1, 3))
+
+        @pl.when(k > NEAR)
+        def _():
+            share(above, (2, 1, 3))
+
+        share(below, (1, 3))
+
+    for b in range(KB):
+        opp_first(b).wait_recv()
+        for way in range(2):
+            opp_block(way, 0, b).start()
 
     far = lax.rem(z + NZ // 2, NZ)
     for b in range(KB):
         for up in (True, False):
             z_half(far, up, b).wait_recv()
-    share(far)
+    share(far, (1, 3, 2))
+
+    for hop in range(1, NEAR):
+        for b in range(KB):
+            for way in range(2):
+                opp_block(way, hop - 1, b).wait_recv()
+                opp_block(way, hop, b).start()
+
+    @pl.loop(NEAR + 1, NZ // 2)
+    def _(k):
+        share(lax.rem(z + k, NZ), (2,), False)
 
     for copy in q_copies:
         copy.wait()
@@ -176,10 +244,15 @@
 
     for d in range(1, NX):
         source = lax.rem(x + NX - d, NX)
-        landed = kv.at[pl.ds(RECV + source * NZ, NZ)]
-        send(picked.at[d - 1], landed, x_send.at[d - 1], x_recv.at[d - 1], at_x(d)).wait()
-
-    @pl.when(x != 0)
+        count = NZ if d != 2 else NZ - 2 * NEAR - 1
+        landed = kv.at[pl.ds(RECV + source * NZ, count)]
+        send(picked.at[d - 1, pl.ds(0, count)], landed, x_send.at[d - 1], x_recv.at[d - 1], at_x(d)).wait()
+
+    for way in range(2):
+        for b in range(KB):
+            opp_block(way, NEAR - 1, b).wait_recv()
+
+    @pl.when((x != 0) & (z == NZ // 2))
     def _():
         glob_copy(1).wait_recv()
 
@@ -203,8 +276,11 @@
         for e in range(5, LIST):
             block = list_ref[i, e]
             shard = (block * 21846) >> 16
-            here = (shard >> 4) == x
-            slots.append(jnp.where(here, (shard & 15) * KB + block - shard * KB, RECV + shard))
+            column, row, off = shard >> 4, shard & (NZ - 1), block - shard * KB
+            ahead = ((row - z + NZ + NEAR) & (NZ - 1))
+            near = (column == lax.rem(x + 2, NX)) & (ahead <= 2 * NEAR)
+            slot = jnp.where(near, OPP + ahead * KB + off, RECV + shard)
+            slots.append(jnp.where(column == x, row * KB + off, slot))
         for e in range(LIST):
             again = jnp.int32(0)
             for f in range(e):
@@ -247,6 +323,11 @@
     own_out.start()
     own_out.wait()
 
+    opp_blocks = kv.at[pl.ds(0, NEAR * KB)]
+    own_blocks = kv.at[pl.ds(0, KB)]
+    for way in range(2):
+        send(opp_blocks, opp_blocks, opp_send.at[way], out_recv, at_z(1 if way == 0 else NZ - 1)).wait_send()
+    send(own_blocks, own_blocks, opp_send.at[2], out_recv, at_x(2)).wait_send()
     for way in range(2):
         up = way == 0
         dev = at_z(1 if up else NZ - 1)
@@ -255,10 +336,13 @@
         half = kv.at[pl.ds(0, KB), pl.ds(0, BLOCK)]
         send(half, half, z_half_send.at[way], z_recv.at[way, 1, 0], dev).wait_send()
 
-    @pl.when(x == 0)
+    @pl.when((x == 0) & (z == 0))
     def _():
         for d in range(1, NX):
             glob_copy(d).wait_send()
+
+    pl.when(up_on)(lambda: glob_on(0).wait_send())
+    pl.when(down_on)(lambda: glob_on(1).wait_send())
 
     everything = out_ref.at[:, pl.ds(0, (NDP - 1) * WIDTH)]
     send(everything, everything, out_send, out_recv, at_p(1)).wait()
@@ -283,12 +367,13 @@
             pltpu.VMEM((NX, NZ, 128), jnp.int32),
             pltpu.VMEM((NX, NZ, 128), jnp.int32),
             pltpu.SMEM((NX, NZ, 128), jnp.int32),
+            pltpu.SemaphoreType.REGULAR,
             dma((2, KB)), dma, dma, dma((NX,)), dma((NX,)), dma, dma((NDP,)), dma((NDP,)),
             dma((2,)), dma((2,)), dma((2, NZ // 2, KB)), dma((2, KB)),
-            dma((NX - 1,)), dma((NX - 1,)), dma((NX,)), dma, dma, dma, dma, dma,
+            dma((NX - 1,)), dma((NX - 1,)), dma((NX,)), dma, dma((3,)), dma((2, NEAR + 1, KB)), dma, dma, dma, dma,
         ],
         compiler_params=pltpu.CompilerParams(
-            collective_id=0, has_side_effects=True, vmem_limit_bytes=48 * 1024 * 1024
+            collective_id=0, has_side_effects=True, vmem_limit_bytes=63 * 1024 * 1024
         ),
         name="gather_attend",
     )(block_list, queries, keys.reshape(KB, BLOCK, HEAD_DIM), values.reshape(KB, BLOCK, HEAD_DIM))

time: 90.5 us -> 86.3 us (0.954)
  local copies, waits for them, and re-layouts: 4.48 us -> 2.06 us
  Pallas kernels: 85.6 us -> 84 us
    unnamed x9 -> x1, local copies, waits for them, and re-layouts: 4.48 us -> 2.06 us
    pallas_call x1, Pallas kernels: 85.6 us -> 84 us  [shards(): pl.pallas_call(kernel, out_shape=jax.ShapeDtypeStruct(queries.shape, quer...]
where the time goes in v2:
time: 86.3 us; the launch traced here: 86.1 us
  Pallas kernels  84 us (97%)
  local copies, waits for them, and re-layouts  2.06 us (2%)
    pallas_call x1, Pallas kernels, shards(): pl.pallas_call(kernel, out_shape=jax.ShapeDtypeStruct(queries.shape, quer...  84 us
    unnamed x1, local copies, waits for them, and re-layouts  2.06 us

profile of v2, /device:TPU:1, one launch (start us, length us, event | category | flops | bytes accessed | tf_op | source)
XLA Modules:
  0.0 86.1 jit_solution(13485068208872611909)
XLA Ops:
  0.0 84.0 %gather_attend.1 = bf16[48,8192]{1,0:T(8,128)(2,1)} custom-call(s32[3,13]{1,0:T(4,128)} %list_ref.1, bf16[48,8192]{1,0:T(8,128)(2,1)} %q_ref.1, bf16[3,128,128]{2,1,0:T(8,128)(2,1)} %bitcast.2, bf16[3,128,128]{2,1,0:T(8,128)(2,1)} %bitcast.3), custom_call_target="tpu_custom_call" | custom-call | tf_op jit(solution)/shard_map/gather_attend/pallas_call | solution.py:355
  84.0 2.1 %copy.6 = bf16[48,8192]{1,0:T(8,128)(2,1)} copy(bf16[48,8192]{1,0:T(8,128)(2,1)} %gather_attend.1) | data formatting | bytes 1572864

commit v3 on v1

v3 whole, which is shorter than its diff:
```python
import math

import jax
import jax.numpy as jnp
from jax import lax
from jax.experimental import pallas as pl
from jax.experimental.pallas import tpu as pltpu
from jax.sharding import PartitionSpec as P

HEAD_DIM = 128
BLOCK = 128
LIST = 13
KB = 3
GROUP = 8
NX, NZ, NDP = 4, 16, 8
TOK = 48
WIDTH = GROUP * HEAD_DIM
SPAN = KB * BLOCK
OWN = NZ * KB
RECV = OWN
GLOB = RECV + NX * NZ
EDGE = GLOB + 2
OPP_AT = (5, 7)
OWN_PLACE, FAR_PLACE = NZ - 2, NZ - 1
GLOB_LAG = 2
NEAR = 2
OPP = EDGE + 1
SLOTS = OPP + (2 * NEAR + 1) * KB
PAIR = 2
STEPS = GROUP // PAIR
MESH = pl.DeviceIdType.MESH


def kernel(list_ref, q_ref, k_ref, v_ref, out_ref, kv, picked, kcat, vcat, qbuf, obuf, ask, asked, asked_s, lower_in,
           load_sem, own_q_sem, own_out_sem, ask_send, ask_recv, asked_sem, q_send, q_recv, z_send, z_recv, x_send, x_recv,
           glob_send, glob_recv, opp_send, opp_recv, edge_send, edge_recv, out_send, out_recv):
    c = lax.axis_index("ctx")
    p = lax.axis_index("dp")
    x = c // NZ
    z = c & (NZ - 1)
    at_x = [{"ctx": ((x + d) & (NX - 1)) * NZ + z, "dp": p} for d in range(NX)]
    at_z = [{"ctx": x * NZ + ((z + d) & (NZ - 1)), "dp": p} for d in (1, NZ - 1)]
    others = [(p + d) & (NDP - 1) for d in range(NDP)]
    at_p = [{"ctx": c, "dp": t} for t in others]

    def send(src, dst, ssem, rsem, dev):
        return pltpu.make_async_remote_copy(
            src_ref=src, dst_ref=dst, send_sem=ssem, recv_sem=rsem, device_id=dev, device_id_type=MESH
        )

    def blocks(slot, count):
        return kv.at[pl.ds(2 * slot, 2 * count)]

    barrier = pltpu.get_barrier_semaphore()
    for dev in at_x[1:] + at_z[1:] + at_p[1:]:
        pl.semaphore_signal(barrier, inc=1, device_id=dev, device_id_type=MESH)

    loads = []
    for b in range(KB):
        part = 2 * (z * KB + b)
        loads.append(pltpu.make_async_copy(k_ref.at[b], kv.at[part], load_sem.at[0, b]))
        loads.append(pltpu.make_async_copy(v_ref.at[b], kv.at[part + 1], load_sem.at[1, b]))
    for copy in loads:
        copy.start()
    own_rows = pl.ds(pl.multiple_of(p * TOK, 16), TOK)
    own_q = pltpu.make_async_copy(
        q_ref.at[:, pl.ds(pl.multiple_of(p * WIDTH, WIDTH), WIDTH)], qbuf.at[own_rows], own_q_sem)
    own_q.start()

    rows = lax.broadcasted_iota(jnp.int32, (NX * NZ, 128), 0) * KB
    wanted = jnp.zeros((NX * NZ, 128), jnp.int32)
    for i in range(KB):
        for e in range(5, LIST):
            off = list_ref[i, e] - rows
            wanted = wanted + jnp.where(off == 1, 1, 0) + jnp.where(off == 2, 2, 0)
    ask[...] = wanted.reshape(NX, NZ, 128)

    for copy in loads:
        copy.wait()
    pl.semaphore_wait(barrier, NX - 1 + 1 + NDP - 1)
    pl.semaphore_signal(lower_in, inc=1, device_id=at_z[0], device_id_type=MESH)

    def z_part(slot, way, k, part):
        half = kv.at[pl.ds(2 * KB * slot + KB * part, KB)]
        return send(half, half, z_send.at[way], z_recv.at[way, k - 1, part], at_z[way])

    for part in range(2):
        z_part(z, 0, 1, part).start()

    asks = []
    for d in range(1, NX):
        asks.append(send(ask.at[(x + d) & (NX - 1)], asked.at[d], ask_send.at[d], ask_recv.at[d], at_x[d]))
        asks[-1].start()

    def opp_shard(way, hop):
        row, step = (-hop, -1) if way == 0 else (hop, 1)
        return send(blocks(OPP + (row + NEAR) * KB, KB), blocks(OPP + (row + step + NEAR) * KB, KB),
                    opp_send.at[way], opp_recv.at[way, hop + 1], at_z[way])

    opp_first = send(blocks(z * KB, KB), blocks(OPP + NEAR * KB, KB), opp_send.at[2], opp_recv.at[0, 0], at_x[2])
    opp_first.start()

    def start_down():
        pl.semaphore_wait(lower_in, 1)
        for part in (1, 0):
            z_part(z, 1, 1, part).start()

    pl.when(z != 0)(start_down)

    for copy in asks:
        copy.wait()
    to_scalars = pltpu.make_async_copy(asked, asked_s, asked_sem)
    to_scalars.start()

    q_copies = []
    for d in range(1, NDP):
        q_copies.append(send(
            q_ref.at[:, pl.ds(pl.multiple_of(others[d] * WIDTH, WIDTH), WIDTH)], qbuf.at[own_rows],
            q_send.at[d], q_recv.at[d], at_p[d]))
        q_copies[-1].start()

    def glob_copy(d, g):
        return send(blocks(g, 1), blocks(GLOB + g, 1), glob_send.at[d], glob_recv.at[g], at_x[d])

    def glob_on(way, g):
        one = blocks(GLOB + g, 1)
        return send(one, one, glob_send.at[way], glob_recv.at[g], at_z[way])

    hops = jnp.where(z > NZ // 2, NZ - z, z)
    up_on = (x != 0) & (z < NZ // 2)
    down_on = (x != 0) & ((z == 0) | (z > NZ // 2 + 1))

    def glob_pass():
        for g in range(2):
            glob_on(0, g).wait_recv()
            pl.when(up_on)(lambda: glob_on(0, g).start())
            pl.when(down_on)(lambda: glob_on(1, g).start())

    def edge_copy(slot, d):
        return send(blocks(slot, 1), blocks(EDGE, 1), edge_send, edge_recv, at_x[d])

    def pick(slot, d, place):
        first, second, third = (kv[pl.ds(2 * (slot * KB + b), 2)] for b in range(KB))
        off = asked_s[NX - d, slot, 0]
        picked[d - 1, pl.ds(2 * place, 2)] = jnp.where(off == 1, second, jnp.where(off == 2, third, first))

    def give(d, place, count):
        send(picked.at[d - 1, pl.ds(2 * place, 2 * count)], blocks(RECV + x * NZ + place, count),
             x_send.at[d - 1], x_recv.at[d - 1], at_x[d]).start()

    to_scalars.wait()

    @pl.when((x == 0) & (z == 0))
    def _():
        for g in range(2):
            for d in range(1, NX):
                glob_copy(d, g).start()

    for d in (1, 3):
        pick(z, d, OWN_PLACE)
        give(d, OWN_PLACE, 1)
    pl.when(z == 0)(start_down)

    @pl.loop(1, NZ // 2)
    def _(k):
        slots = ((z + NZ - k) & (NZ - 1), (z + k) & (NZ - 1))
        for turn in range(2):
            for way in range(2):
                part = turn if way == 0 else 1 - turn
                z_part(slots[way], way, k, part).wait_recv()
                if part == way:
                    z_part(slots[way], way, k + 1, part).start()
                else:
                    pl.when(k < NZ // 2 - 1)(lambda: z_part(slots[way], way, k + 1, part).start())

        def share(d):
            for way in range(2):
                pick(slots[way], d, 2 * (k - 1) + way)
            give(d, 2 * (k - 1), 2)

        pl.when(k > NEAR)(lambda: share(2))
        share(1)
        share(3)

        @pl.when((z == 0) & (k == 1))
        def _():
            edge_copy(OWN - 1, 1).start()

        @pl.when((z == NZ - 1) & (k == 1))
        def _():
            edge_copy(0, NX - 1).start()

        pl.when((x != 0) & (hops == k - GLOB_LAG))(glob_pass)

        for hop in range(NEAR):
            @pl.when(k == OPP_AT[hop])
            def _():
                if hop == 0:
                    opp_first.wait_recv()
                for way in range(2):
                    if hop > 0:
                        opp_shard(way, hop - 1).wait_recv()
                    opp_shard(way, hop).start()

    far = (z + NZ // 2) & (NZ - 1)
    for way in range(2):
        z_part(far, way, NZ // 2, way).wait_recv()
    for d in (2, 1, 3):
        pick(far, d, FAR_PLACE)
        give(d, FAR_PLACE, 1)
    pl.when((x != 0) & (hops > NZ // 2 - 1 - GLOB_LAG))(glob_pass)

    for copy in q_copies:
        copy.wait()
    own_q.wait()

    for d in (1, 3, 2):
        count = NZ if d != 2 else NZ - 2 * NEAR - 1
        landed = blocks(RECV + ((x - d) & (NX - 1)) * NZ, count)
        send(picked.at[d - 1, pl.ds(0, 2 * count)], landed, x_send.at[d - 1], x_recv.at[d - 1], at_x[d]).wait()

    if NEAR:
        for way in range(2):
            opp_shard(way, NEAR - 1).wait_recv()
    else:
        opp_first.wait_recv()

    @pl.when((z == 0) | (z == NZ - 1))
    def _():
        edge_copy(0, 1).wait()

    for i in range(KB):
        slots = []
        if i == 0:
            slots.append(jnp.where(z == 0, EDGE, z * KB - 1))
        else:
            slots.append(z * KB + i - 1)
        slots.append(z * KB + i)
        if i == KB - 1:
            slots.append(jnp.where(z == NZ - 1, EDGE, z * KB + KB))
        else:
            slots.append(z * KB + i + 1)
        for g in range(2):
            slots.append(jnp.where(x == 0, g, GLOB + g))
        for e in range(5, LIST):
            block = list_ref[i, e]
            shard = (block * 21846) >> 16
            column, row, off = shard >> 4, shard & (NZ - 1), block - shard * KB
            ahead = ((row - z + NZ + NEAR) & (NZ - 1))
            ahead = (row - z) & (NZ - 1)
            place = jnp.where(ahead > NZ // 2, 2 * (NZ - 1 - ahead), 2 * ahead - 1)
            place = jnp.where(ahead == 0, OWN_PLACE, jnp.where(ahead == NZ // 2, FAR_PLACE, place))
            ahead = (ahead + NEAR) & (NZ - 1)
            near = (column == ((x + 2) & (NX - 1))) & (ahead <= 2 * NEAR)
            slot = jnp.where(near, OPP + ahead * KB + off, RECV + column * NZ + place)
            slots.append(jnp.where(column == x, row * KB + off, slot))
        for e in range(LIST):
            again = jnp.int32(0)
            for f in range(e):
                again = again | jnp.where(list_ref[i, e] == list_ref[i, f], 1, 0)
            keep = jnp.where(again == 1, 0.0, 1.0)
            both = kv[pl.ds(2 * slots[e], 2)]
            kcat[i, pl.ds(e * BLOCK, BLOCK)] = both[0]
            mask = jnp.full((BLOCK, HEAD_DIM), keep, jnp.float32).astype(jnp.bfloat16)
            vcat[i, pl.ds(e * BLOCK, BLOCK), pl.ds(0, HEAD_DIM)] = both[1] * mask
            vcat[i, pl.ds(e * BLOCK, BLOCK), pl.ds(HEAD_DIM, HEAD_DIM)] = mask

    factor = math.log2(math.e) / math.sqrt(HEAD_DIM)

    def out_copy(d, step):
        return send(
            obuf.at[pl.ds(pl.multiple_of(others[d] * TOK, 16), TOK), pl.ds(pl.multiple_of(step * PAIR * HEAD_DIM, 256), PAIR * HEAD_DIM)],
            out_ref.at[:, pl.ds(pl.multiple_of(p * WIDTH + step * PAIR * HEAD_DIM, 256), PAIR * HEAD_DIM)],
            out_send, out_recv, at_p[d])

    @pl.loop(0, STEPS)
    def _(step):
        for i in range(KB):
            tok = pl.ds(i * BLOCK, BLOCK)
            cols = [pl.ds(pl.multiple_of((step * PAIR + h) * HEAD_DIM, HEAD_DIM), HEAD_DIM) for h in range(PAIR)]
            q = jnp.concatenate([qbuf[tok, col] for col in cols], axis=0)
            scores = lax.dot_general(q, kcat[i], (((1,), (1,)), ((), ())), preferred_element_type=jnp.float32)
            row_max = jnp.max(scores, axis=-1, keepdims=True)
            unnormed = jnp.exp2((scores - row_max) * factor).astype(jnp.bfloat16)
            result = jnp.dot(unnormed, vcat[i], preferred_element_type=jnp.float32)
            result = (result[:, :HEAD_DIM] / result[:, HEAD_DIM:]).astype(jnp.bfloat16)
            for h in range(PAIR):
                obuf[tok, cols[h]] = result[h * BLOCK:(h + 1) * BLOCK]
        for d in range(1, NDP):
            out_copy(d, step).start()

    own_out = pltpu.make_async_copy(
        obuf.at[pl.ds(pl.multiple_of(p * TOK, 16), TOK)],
        out_ref.at[:, pl.ds(pl.multiple_of(p * WIDTH, WIDTH), WIDTH)], own_out_sem)
    own_out.start()
    own_out.wait()

    for way in range(2):
        if NEAR:
            passed = blocks(0, NEAR * KB)
            send(passed, passed, opp_send.at[way], out_recv, at_z[way]).wait_send()
        sent = kv.at[pl.ds(0, (NZ - 1) * KB)]
        send(sent, sent, z_send.at[way], out_recv, at_z[way]).wait_send()
    opp_first.wait_send()

    @pl.when((x == 0) & (z == 0))
    def _():
        both = blocks(0, 2)
        for d in range(1, NX):
            send(both, both, glob_send.at[d], out_recv, at_x[d]).wait_send()

    def glob_sent(way):
        both = blocks(GLOB, 2)
        send(both, both, glob_send.at[way], out_recv, at_z[way]).wait_send()

    pl.when(up_on)(lambda: glob_sent(0))
    pl.when(down_on)(lambda: glob_sent(1))

    everything = out_ref.at[:, pl.ds(0, (NDP - 1) * WIDTH)]
    send(everything, everything, out_send, out_recv, at_p[1]).wait()


def shards(queries, keys, values, block_list):
    dma = pltpu.SemaphoreType.DMA
    bf16 = jnp.bfloat16
    hbm = pl.BlockSpec(memory_space=pl.ANY)
    return pl.pallas_call(
        kernel,
        out_shape=jax.ShapeDtypeStruct(queries.shape, queries.dtype),
        in_specs=[pl.BlockSpec(memory_space=pltpu.SMEM), hbm, hbm, hbm],
        out_specs=hbm,
        scratch_shapes=[
            pltpu.VMEM((2 * SLOTS, BLOCK, HEAD_DIM), bf16),
            pltpu.VMEM((NX - 1, 2 * NZ, BLOCK, HEAD_DIM), bf16),
            pltpu.VMEM((KB, LIST * BLOCK, HEAD_DIM), bf16),
            pltpu.VMEM((KB, LIST * BLOCK, 2 * HEAD_DIM), bf16),
            pltpu.VMEM((SPAN, WIDTH), bf16),
            pltpu.VMEM((SPAN, WIDTH), bf16),
            pltpu.VMEM((NX, NZ, 128), jnp.int32),
            pltpu.VMEM((NX, NZ, 128), jnp.int32),
            pltpu.SMEM((NX, NZ, 128), jnp.int32),
            pltpu.SemaphoreType.REGULAR,
            dma((2, KB)), dma, dma, dma((NX,)), dma((NX,)), dma, dma((NDP,)), dma((NDP,)),
            dma((2,)), dma((2, NZ // 2, 2)),
            dma((NX - 1,)), dma((NX - 1,)), dma((NX,)), dma((2,)), dma((3,)), dma((2, NEAR + 1)), dma, dma, dma, dma,
        ],
        compiler_params=pltpu.CompilerParams(
            collective_id=0, has_side_effects=True, vmem_limit_bytes=63 * 1024 * 1024
        ),
        name="gather_attend",
    )(block_list, queries, keys.reshape(KB, BLOCK, HEAD_DIM), values.reshape(KB, BLOCK, HEAD_DIM))


def solution(mesh):
    in_specs = (P(("ctx", "dp"), None), P("ctx", "dp"), P("ctx", "dp"), P("ctx", None))
    out_specs = P(("ctx", "dp"), None)
    return jax.shard_map(shards, mesh=mesh, in_specs=in_specs, out_specs=out_specs, check_vma=False)
```

time: 90.5 us -> 80.7 us (0.89)
  Pallas kernels: 85.6 us -> 78.4 us
  local copies, waits for them, and re-layouts: 4.48 us -> 2.06 us
    pallas_call x1, Pallas kernels: 85.6 us -> 78.4 us  [shards(): pl.pallas_call(kernel, out_shape=jax.ShapeDtypeStruct(queries.shape, quer...]
    unnamed x9 -> x1, local copies, waits for them, and re-layouts: 4.48 us -> 2.06 us
where the time goes in v3:
time: 80.7 us; the launch traced here: 80.5 us
  Pallas kernels  78.4 us (97%)
  local copies, waits for them, and re-layouts  2.06 us (3%)
    pallas_call x1, Pallas kernels, shards(): pl.pallas_call(kernel, out_shape=jax.ShapeDtypeStruct(queries.shape, quer...  78.4 us
    unnamed x1, local copies, waits for them, and re-layouts  2.06 us

profile of v3, /device:TPU:1, one launch (start us, length us, event | category | flops | bytes accessed | tf_op | source)
XLA Modules:
  0.0 80.5 jit_solution(13311318373692062773)
XLA Ops:
  0.0 78.4 %gather_attend.1 = bf16[48,8192]{1,0:T(8,128)(2,1)} custom-call(s32[3,13]{1,0:T(4,128)} %list_ref.1, bf16[48,8192]{1,0:T(8,128)(2,1)} %q_ref.1, bf16[3,128,128]{2,1,0:T(8,128)(2,1)} %bitcast.2, bf16[3,128,128]{2,1,0:T(8,128)(2,1)} %bitcast.3), custom_call_target="tpu_custom_call" | custom-call | tf_op jit(solution)/shard_map/gather_attend/pallas_call | solution.py:327
  78.4 2.1 %copy.6 = bf16[48,8192]{1,0:T(8,128)(2,1)} copy(bf16[48,8192]{1,0:T(8,128)(2,1)} %gather_attend.1) | data formatting | bytes 1572864

commit v4 on v3

--- a/solution.py
+++ b/solution.py
@@ -23,6 +23,7 @@
 OPP_AT = (5, 7)
 OWN_PLACE, FAR_PLACE = NZ - 2, NZ - 1
 GLOB_LAG = 2
+LATE = 7
 NEAR = 2
 OPP = EDGE + 1
 SLOTS = OPP + (2 * NEAR + 1) * KB
@@ -31,8 +32,8 @@
 MESH = pl.DeviceIdType.MESH
 
 
-def kernel(list_ref, q_ref, k_ref, v_ref, out_ref, kv, picked, kcat, vcat, qbuf, obuf, ask, asked, asked_s, lower_in,
-           load_sem, own_q_sem, own_out_sem, ask_send, ask_recv, asked_sem, q_send, q_recv, z_send, z_recv, x_send, x_recv,
+def kernel(lists, q_ref, k_ref, v_ref, out_ref, kv, given_v, picked, kcat, vcat, weights, qbuf, obuf, ask, asked, asked_s, list_ref, lower_in,
+           list_sem, load_sem, own_q_sem, own_out_sem, ask_send, ask_recv, asked_sem, q_send, q_recv, z_send, z_recv, x_send, x_recv,
            glob_send, glob_recv, opp_send, opp_recv, edge_send, edge_recv, out_send, out_recv):
     c = lax.axis_index("ctx")
     p = lax.axis_index("dp")
@@ -49,17 +50,18 @@
         )
 
     def blocks(slot, count):
-        return kv.at[pl.ds(2 * slot, 2 * count)]
-
+        return kv.at[pl.ds(slot, count)]
+
+    list_copy = pltpu.make_async_copy(lists, list_ref, list_sem)
+    list_copy.start()
     barrier = pltpu.get_barrier_semaphore()
     for dev in at_x[1:] + at_z[1:] + at_p[1:]:
         pl.semaphore_signal(barrier, inc=1, device_id=dev, device_id_type=MESH)
 
     loads = []
     for b in range(KB):
-        part = 2 * (z * KB + b)
-        loads.append(pltpu.make_async_copy(k_ref.at[b], kv.at[part], load_sem.at[0, b]))
-        loads.append(pltpu.make_async_copy(v_ref.at[b], kv.at[part + 1], load_sem.at[1, b]))
+        loads.append(pltpu.make_async_copy(k_ref.at[b], kv.at[z * KB + b, 0], load_sem.at[0, b]))
+        loads.append(pltpu.make_async_copy(v_ref.at[b], kv.at[z * KB + b, 1], load_sem.at[1, b]))
     for copy in loads:
         copy.start()
     own_rows = pl.ds(pl.multiple_of(p * TOK, 16), TOK)
@@ -67,6 +69,7 @@
         q_ref.at[:, pl.ds(pl.multiple_of(p * WIDTH, WIDTH), WIDTH)], qbuf.at[own_rows], own_q_sem)
     own_q.start()
 
+    list_copy.wait()
     rows = lax.broadcasted_iota(jnp.int32, (NX * NZ, 128), 0) * KB
     wanted = jnp.zeros((NX * NZ, 128), jnp.int32)
     for i in range(KB):
@@ -81,7 +84,7 @@
     pl.semaphore_signal(lower_in, inc=1, device_id=at_z[0], device_id_type=MESH)
 
     def z_part(slot, way, k, part):
-        half = kv.at[pl.ds(2 * KB * slot + KB * part, KB)]
+        half = kv.at[pl.ds(KB * slot, KB), part]
         return send(half, half, z_send.at[way], z_recv.at[way, k - 1, part], at_z[way])
 
     for part in range(2):
@@ -111,6 +114,53 @@
         copy.wait()
     to_scalars = pltpu.make_async_copy(asked, asked_s, asked_sem)
     to_scalars.start()
+
+    def glob_copy(d, g):
+        return send(blocks(g, 1), blocks(GLOB + g, 1), glob_send.at[d], glob_recv.at[g], at_x[d])
+
+    def glob_on(way, g):
+        one = blocks(GLOB + g, 1)
+        return send(one, one, glob_send.at[way], glob_recv.at[g], at_z[way])
+
+    hops = jnp.where(z > NZ // 2, NZ - z, z)
+    up_on = (x != 0) & (z < NZ // 2)
+    down_on = (x != 0) & ((z == 0) | (z > NZ // 2 + 1))
+
+    def glob_pass():
+        for g in range(2):
+            glob_on(0, g).wait_recv()
+            pl.when(up_on)(lambda: glob_on(0, g).start())
+            pl.when(down_on)(lambda: glob_on(1, g).start())
+
+    def edge_copy(slot, d):
+        return send(blocks(slot, 1), blocks(EDGE, 1), edge_send, edge_recv, at_x[d])
+
+    def pick(slot, d, place):
+        first, second, third = (kv[slot * KB + b] for b in range(KB))
+        off = asked_s[NX - d, slot, 0]
+        picked[d - 1, place] = jnp.where(off == 1, second, jnp.where(off == 2, third, first))
+
+    def give(d, place, count, parts=(0, 1)):
+        for part in parts:
+            if part == 0:
+                target = kv.at[pl.ds(RECV + x * NZ + place, count), 0]
+            else:
+                target = given_v.at[pl.ds(x * NZ + place, count)]
+            send(picked.at[d - 1, pl.ds(place, count), part], target,
+                 x_send.at[part, d - 1], x_recv.at[part, d - 1], at_x[d]).start()
+
+    to_scalars.wait()
+
+    @pl.when((x == 0) & (z == 0))
+    def _():
+        for g in range(2):
+            for d in range(1, NX):
+                glob_copy(d, g).start()
+
+    for d in (1, 3):
+        pick(z, d, OWN_PLACE)
+        give(d, OWN_PLACE, 1)
+    pl.when(z == 0)(start_down)
 
     q_copies = []
     for d in range(1, NDP):
@@ -118,48 +168,6 @@
             q_ref.at[:, pl.ds(pl.multiple_of(others[d] * WIDTH, WIDTH), WIDTH)], qbuf.at[own_rows],
             q_send.at[d], q_recv.at[d], at_p[d]))
         q_copies[-1].start()
-
-    def glob_copy(d, g):
-        return send(blocks(g, 1), blocks(GLOB + g, 1), glob_send.at[d], glob_recv.at[g], at_x[d])
-
-    def glob_on(way, g):
-        one = blocks(GLOB + g, 1)
-        return send(one, one, glob_send.at[way], glob_recv.at[g], at_z[way])
-
-    hops = jnp.where(z > NZ // 2, NZ - z, z)
-    up_on = (x != 0) & (z < NZ // 2)
-    down_on = (x != 0) & ((z == 0) | (z > NZ // 2 + 1))
-
-    def glob_pass():
-        for g in range(2):
-            glob_on(0, g).wait_recv()
-            pl.when(up_on)(lambda: glob_on(0, g).start())
-            pl.when(down_on)(lambda: glob_on(1, g).start())
-
-    def edge_copy(slot, d):
-        return send(blocks(slot, 1), blocks(EDGE, 1), edge_send, edge_recv, at_x[d])
-
-    def pick(slot, d, place):
-        first, second, third = (kv[pl.ds(2 * (slot * KB + b), 2)] for b in range(KB))
-        off = asked_s[NX - d, slot, 0]
-        picked[d - 1, pl.ds(2 * place, 2)] = jnp.where(off == 1, second, jnp.where(off == 2, third, first))
-
-    def give(d, place, count):
-        send(picked.at[d - 1, pl.ds(2 * place, 2 * count)], blocks(RECV + x * NZ + place, count),
-             x_send.at[d - 1], x_recv.at[d - 1], at_x[d]).start()
-
-    to_scalars.wait()
-
-    @pl.when((x == 0) & (z == 0))
-    def _():
-        for g in range(2):
-            for d in range(1, NX):
-                glob_copy(d, g).start()
-
-    for d in (1, 3):
-        pick(z, d, OWN_PLACE)
-        give(d, OWN_PLACE, 1)
-    pl.when(z == 0)(start_down)
 
     @pl.loop(1, NZ // 2)
     def _(k):
@@ -176,7 +184,8 @@
         def share(d):
             for way in range(2):
                 pick(slots[way], d, 2 * (k - 1) + way)
-            give(d, 2 * (k - 1), 2)
+            give(d, 2 * (k - 1), 2, (0,))
+            pl.when(k < LATE)(lambda: give(d, 2 * (k - 1), 2, (1,)))
 
         pl.when(k > NEAR)(lambda: share(2))
         share(1)
@@ -207,17 +216,28 @@
         z_part(far, way, NZ // 2, way).wait_recv()
     for d in (2, 1, 3):
         pick(far, d, FAR_PLACE)
-        give(d, FAR_PLACE, 1)
+        give(d, FAR_PLACE, 1, (0,))
+
+    @pl.loop(LATE, NZ // 2)
+    def _(k):
+        for d in (2, 1, 3):
+            give(d, 2 * (k - 1), 2, (1,))
+
+    for d in (2, 1, 3):
+        give(d, FAR_PLACE, 1, (1,))
     pl.when((x != 0) & (hops > NZ // 2 - 1 - GLOB_LAG))(glob_pass)
 
     for copy in q_copies:
         copy.wait()
     own_q.wait()
 
-    for d in (1, 3, 2):
-        count = NZ if d != 2 else NZ - 2 * NEAR - 1
-        landed = blocks(RECV + ((x - d) & (NX - 1)) * NZ, count)
-        send(picked.at[d - 1, pl.ds(0, 2 * count)], landed, x_send.at[d - 1], x_recv.at[d - 1], at_x[d]).wait()
+    def wait_given(part):
+        for d in (1, 3, 2):
+            count = NZ if d != 2 else NZ - 2 * NEAR - 1
+            first = ((x - d) & (NX - 1)) * NZ
+            landed = kv.at[pl.ds(RECV + first, count), 0] if part == 0 else given_v.at[pl.ds(first, count)]
+            send(picked.at[d - 1, pl.ds(0, count), part], landed, x_send.at[part, d - 1], x_recv.at[part, d - 1],
+                 at_x[d]).wait()
 
     if NEAR:
         for way in range(2):
@@ -229,8 +249,11 @@
     def _():
         edge_copy(0, 1).wait()
 
+    wait_given(0)
+
+    every = []
     for i in range(KB):
-        slots = []
+        slots, given = [], [None] * 5
         if i == 0:
             slots.append(jnp.where(z == 0, EDGE, z * KB - 1))
         else:
@@ -254,18 +277,38 @@
             near = (column == ((x + 2) & (NX - 1))) & (ahead <= 2 * NEAR)
             slot = jnp.where(near, OPP + ahead * KB + off, RECV + column * NZ + place)
             slots.append(jnp.where(column == x, row * KB + off, slot))
+            given.append((jnp.where(near | (column == x), 0, 1), column * NZ + place))
+        every.append((slots, given))
+        for e in range(LIST):
+            kcat[i, pl.ds(e * BLOCK, BLOCK)] = kv[slots[e], 0]
+
+    factor = math.log2(math.e) / math.sqrt(HEAD_DIM)
+
+    def head_cols(step):
+        return [pl.ds(pl.multiple_of((step * PAIR + h) * HEAD_DIM, HEAD_DIM), HEAD_DIM) for h in range(PAIR)]
+
+    @pl.loop(0, STEPS)
+    def _(step):
+        for i in range(KB):
+            q = jnp.concatenate([qbuf[pl.ds(i * BLOCK, BLOCK), col] for col in head_cols(step)], axis=0)
+            scores = lax.dot_general(q, kcat[i], (((1,), (1,)), ((), ())), preferred_element_type=jnp.float32)
+            row_max = jnp.max(scores, axis=-1, keepdims=True)
+            weights[step, i] = jnp.exp2((scores - row_max) * factor).astype(jnp.bfloat16)
+
+    wait_given(1)
+    for i in range(KB):
         for e in range(LIST):
             again = jnp.int32(0)
             for f in range(e):
                 again = again | jnp.where(list_ref[i, e] == list_ref[i, f], 1, 0)
             keep = jnp.where(again == 1, 0.0, 1.0)
-            both = kv[pl.ds(2 * slots[e], 2)]
-            kcat[i, pl.ds(e * BLOCK, BLOCK)] = both[0]
             mask = jnp.full((BLOCK, HEAD_DIM), keep, jnp.float32).astype(jnp.bfloat16)
-            vcat[i, pl.ds(e * BLOCK, BLOCK), pl.ds(0, HEAD_DIM)] = both[1] * mask
+            slots, given = every[i]
+            rows = kv[slots[e], 1]
+            if given[e] is not None:
+                rows = jnp.where(given[e][0] == 1, given_v[given[e][1]], rows)
+            vcat[i, pl.ds(e * BLOCK, BLOCK), pl.ds(0, HEAD_DIM)] = rows * mask
             vcat[i, pl.ds(e * BLOCK, BLOCK), pl.ds(HEAD_DIM, HEAD_DIM)] = mask
-
-    factor = math.log2(math.e) / math.sqrt(HEAD_DIM)
 
     def out_copy(d, step):
         return send(
@@ -276,16 +319,10 @@
     @pl.loop(0, STEPS)
     def _(step):
         for i in range(KB):
-            tok = pl.ds(i * BLOCK, BLOCK)
-            cols = [pl.ds(pl.multiple_of((step * PAIR + h) * HEAD_DIM, HEAD_DIM), HEAD_DIM) for h in range(PAIR)]
-            q = jnp.concatenate([qbuf[tok, col] for col in cols], axis=0)
-            scores = lax.dot_general(q, kcat[i], (((1,), (1,)), ((), ())), preferred_element_type=jnp.float32)
-            row_max = jnp.max(scores, axis=-1, keepdims=True)
-            unnormed = jnp.exp2((scores - row_max) * factor).astype(jnp.bfloat16)
-            result = jnp.dot(unnormed, vcat[i], preferred_element_type=jnp.float32)
+            result = jnp.dot(weights[step, i], vcat[i], preferred_element_type=jnp.float32)
             result = (result[:, :HEAD_DIM] / result[:, HEAD_DIM:]).astype(jnp.bfloat16)
-            for h in range(PAIR):
-                obuf[tok, cols[h]] = result[h * BLOCK:(h + 1) * BLOCK]
+            for h, col in enumerate(head_cols(step)):
+                obuf[pl.ds(i * BLOCK, BLOCK), col] = result[h * BLOCK:(h + 1) * BLOCK]
         for d in range(1, NDP):
             out_copy(d, step).start()
 
@@ -299,7 +336,7 @@
         if NEAR:
             passed = blocks(0, NEAR * KB)
             send(passed, passed, opp_send.at[way], out_recv, at_z[way]).wait_send()
-        sent = kv.at[pl.ds(0, (NZ - 1) * KB)]
+        sent = kv.at[pl.ds(0, (NZ - 1) * KB), 0]
         send(sent, sent, z_send.at[way], out_recv, at_z[way]).wait_send()
     opp_first.wait_send()
 
@@ -327,22 +364,25 @@
     return pl.pallas_call(
         kernel,
         out_shape=jax.ShapeDtypeStruct(queries.shape, queries.dtype),
-        in_specs=[pl.BlockSpec(memory_space=pltpu.SMEM), hbm, hbm, hbm],
+        in_specs=[hbm] * 4,
         out_specs=hbm,
         scratch_shapes=[
-            pltpu.VMEM((2 * SLOTS, BLOCK, HEAD_DIM), bf16),
-            pltpu.VMEM((NX - 1, 2 * NZ, BLOCK, HEAD_DIM), bf16),
+            pltpu.VMEM((SLOTS, 2, BLOCK, HEAD_DIM), bf16),
+            pltpu.VMEM((NX * NZ, BLOCK, HEAD_DIM), bf16),
+            pltpu.VMEM((NX - 1, NZ, 2, BLOCK, HEAD_DIM), bf16),
             pltpu.VMEM((KB, LIST * BLOCK, HEAD_DIM), bf16),
             pltpu.VMEM((KB, LIST * BLOCK, 2 * HEAD_DIM), bf16),
+            pltpu.VMEM((STEPS, KB, PAIR * BLOCK, LIST * BLOCK), bf16),
             pltpu.VMEM((SPAN, WIDTH), bf16),
             pltpu.VMEM((SPAN, WIDTH), bf16),
             pltpu.VMEM((NX, NZ, 128), jnp.int32),
             pltpu.VMEM((NX, NZ, 128), jnp.int32),
             pltpu.SMEM((NX, NZ, 128), jnp.int32),
+            pltpu.SMEM((KB, LIST), jnp.int32),
             pltpu.SemaphoreType.REGULAR,
-            dma((2, KB)), dma, dma, dma((NX,)), dma((NX,)), dma, dma((NDP,)), dma((NDP,)),
+            dma, dma((2, KB)), dma, dma, dma((NX,)), dma((NX,)), dma, dma((NDP,)), dma((NDP,)),
             dma((2,)), dma((2, NZ // 2, 2)),
-            dma((NX - 1,)), dma((NX - 1,)), dma((NX,)), dma((2,)), dma((3,)), dma((2, NEAR + 1)), dma, dma, dma, dma,
+            dma((2, NX - 1)), dma((2, NX - 1)), dma((NX,)), dma((2,)), dma((3,)), dma((2, NEAR + 1)), dma, dma, dma, dma,
         ],
         compiler_params=pltpu.CompilerParams(
             collective_id=0, has_side_effects=True, vmem_limit_bytes=63 * 1024 * 1024

time: 80.7 us -> 79.1 us (0.980)
  Pallas kernels: 78.4 us -> 76.8 us
    pallas_call x1, Pallas kernels: 78.4 us -> 76.8 us  [shards(): pl.pallas_call(kernel, out_shape=jax.ShapeDtypeStruct(queries.shape, quer...]
where the time goes in v4:
time: 79.1 us; the launch traced here: 78.9 us
  Pallas kernels  76.8 us (97%)
  local copies, waits for them, and re-layouts  2.06 us (3%)
    pallas_call x1, Pallas kernels, shards(): pl.pallas_call(kernel, out_shape=jax.ShapeDtypeStruct(queries.shape, quer...  76.8 us
    unnamed x1, local copies, waits for them, and re-layouts  2.06 us

profile of v4, /device:TPU:1, one launch (start us, length us, event | category | flops | bytes accessed | tf_op | source)
XLA Modules:
  0.0 78.9 jit_solution(8508086667524795343)
XLA Ops:
  0.0 76.8 %gather_attend.1 = bf16[48,8192]{1,0:T(8,128)(2,1)} custom-call(s32[3,13]{1,0:T(4,128)} %lists.1, bf16[48,8192]{1,0:T(8,128)(2,1)} %q_ref.1, bf16[3,128,128]{2,1,0:T(8,128)(2,1)} %bitcast.2, bf16[3,128,128]{2,1,0:T(8,128)(2,1)} %bitcast.3), custom_call_target="tpu_custom_call" | custom-call | tf_op jit(solution)/shard_map/gather_attend/pallas_call | solution.py:364
  76.8 2.1 %copy.6 = bf16[48,8192]{1,0:T(8,128)(2,1)} copy(bf16[48,8192]{1,0:T(8,128)(2,1)} %gather_attend.1) | data formatting | bytes 1572864

commit v5 on v4

--- a/solution.py
+++ b/solution.py
@@ -22,7 +22,7 @@
 EDGE = GLOB + 2
 OPP_AT = (5, 7)
 OWN_PLACE, FAR_PLACE = NZ - 2, NZ - 1
-GLOB_LAG = 2
+GLOB_LAG = 3
 LATE = 7
 NEAR = 2
 OPP = EDGE + 1
@@ -252,6 +252,10 @@
     wait_given(0)
 
     every = []
+
+    def fill(keep):
+        return jnp.full((BLOCK, HEAD_DIM), keep, jnp.float32).astype(jnp.bfloat16)
+
     for i in range(KB):
         slots, given = [], [None] * 5
         if i == 0:
@@ -278,7 +282,16 @@
             slot = jnp.where(near, OPP + ahead * KB + off, RECV + column * NZ + place)
             slots.append(jnp.where(column == x, row * KB + off, slot))
             given.append((jnp.where(near | (column == x), 0, 1), column * NZ + place))
-        every.append((slots, given))
+        keeps = []
+        for e in range(LIST):
+            again = jnp.int32(0)
+            for f in range(e):
+                again = again | jnp.where(list_ref[i, e] == list_ref[i, f], 1, 0)
+            keeps.append(jnp.where(again == 1, 0.0, 1.0))
+            vcat[i, pl.ds(e * BLOCK, BLOCK), pl.ds(HEAD_DIM, HEAD_DIM)] = fill(keeps[e])
+        for e in range(5):
+            vcat[i, pl.ds(e * BLOCK, BLOCK), pl.ds(0, HEAD_DIM)] = kv[slots[e], 1] * fill(keeps[e])
+        every.append((slots, given, keeps))
         for e in range(LIST):
             kcat[i, pl.ds(e * BLOCK, BLOCK)] = kv[slots[e], 0]
 
@@ -297,18 +310,10 @@
 
     wait_given(1)
     for i in range(KB):
-        for e in range(LIST):
-            again = jnp.int32(0)
-            for f in range(e):
-                again = again | jnp.where(list_ref[i, e] == list_ref[i, f], 1, 0)
-            keep = jnp.where(again == 1, 0.0, 1.0)
-            mask = jnp.full((BLOCK, HEAD_DIM), keep, jnp.float32).astype(jnp.bfloat16)
-            slots, given = every[i]
-            rows = kv[slots[e], 1]
-            if given[e] is not None:
-                rows = jnp.where(given[e][0] == 1, given_v[given[e][1]], rows)
-            vcat[i, pl.ds(e * BLOCK, BLOCK), pl.ds(0, HEAD_DIM)] = rows * mask
-            vcat[i, pl.ds(e * BLOCK, BLOCK), pl.ds(HEAD_DIM, HEAD_DIM)] = mask
+        slots, given, keeps = every[i]
+        for e in range(5, LIST):
+            rows = jnp.where(given[e][0] == 1, given_v[given[e][1]], kv[slots[e], 1])
+            vcat[i, pl.ds(e * BLOCK, BLOCK), pl.ds(0, HEAD_DIM)] = rows * fill(keeps[e])
 
     def out_copy(d, step):
         return send(

time: 79.1 us -> 78.5 us (level)
  no operation moved by 1% of the time
where the time goes in v5:
time: 78.5 us; the launch traced here: 78.3 us
  Pallas kernels  76.2 us (97%)
  local copies, waits for them, and re-layouts  2.06 us (3%)
    pallas_call x1, Pallas kernels, shards(): pl.pallas_call(kernel, out_shape=jax.ShapeDtypeStruct(queries.shape, quer...  76.2 us
    unnamed x1, local copies, waits for them, and re-layouts  2.06 us

profile of v5, /device:TPU:1, one launch (start us, length us, event | category | flops | bytes accessed | tf_op | source)
XLA Modules:
  0.0 78.3 jit_solution(14755226305904625185)
XLA Ops:
  0.0 76.2 %gather_attend.1 = bf16[48,8192]{1,0:T(8,128)(2,1)} custom-call(s32[3,13]{1,0:T(4,128)} %lists.1, bf16[48,8192]{1,0:T(8,128)(2,1)} %q_ref.1, bf16[3,128,128]{2,1,0:T(8,128)(2,1)} %bitcast.2, bf16[3,128,128]{2,1,0:T(8,128)(2,1)} %bitcast.3), custom_call_target="tpu_custom_call" | custom-call | tf_op jit(solution)/shard_map/gather_attend/pallas_call | solution.py:369
  76.2 2.1 %copy.6 = bf16[48,8192]{1,0:T(8,128)(2,1)} copy(bf16[48,8192]{1,0:T(8,128)(2,1)} %gather_attend.1) | data formatting | bytes 1572864
